TPU v7x, 32 devices: a whole 2x2x4 slice. The times are simulated.
32 devices in a mesh: row: 2 (over core), col: 16 (over z, y, x).
Axes of the slice: x: 2, y: 2, z: 4, core: 2. Of those that a mesh axis runs over, the one named last changes fastest.
Arguments:
- basis_out: float32 [16384, 16384], P('row', 'col'), may hold values from -0.046875 to 0.046875
- basis_in: float32 [16384, 16384], P('col', 'row'), may hold values from -0.046875 to 0.046875
- eig_damped: float32 [16384, 16384], P('col', 'row'), may hold values from 0.5 to 8
- query_left: bfloat16 [16384, 256], P(('row', 'col')), may hold values from -0.375 to 0.375
- query_right: bfloat16 [16384, 256], P('col'), may hold values from -6 to 6
- train_left: bfloat16 [16384, 512], P(('row', 'col')), may hold values from -0.046875 to 0.046875
- train_right: bfloat16 [16384, 512], P('col'), may hold values from -0.046875 to 0.046875
Outputs:
- response: float32 [16384, 512], P(('row', 'col'))
- scores: float32 [512], replicated
All inputs are finite; a program needn't handle non-finite values.
Results may differ from a plain program's by a relative error of at most 0.0003.
Values may be sent and summed in bfloat16 or wider, within the bound.
A program may use at most 256 MiB of HBM per device.

v0:
```python
import jax
import jax.numpy as jnp
from jax import lax
from jax.sharding import PartitionSpec as P


def dot_first(left, right):
    return lax.dot_general(
        left,
        right,
        (((0,), (0,)), ((), ())),
        precision=lax.Precision.HIGHEST,
        preferred_element_type=jnp.float32,
    )


def dot_last(left, right):
    return lax.dot_general(
        left,
        right,
        (((1,), (1,)), ((), ())),
        precision=lax.Precision.HIGHEST,
        preferred_element_type=jnp.float32,
    )


def dot_plain(left, right):
    return jnp.dot(left, right, precision=lax.Precision.HIGHEST, preferred_element_type=jnp.float32)


def body(basis_out, basis_in, eig_damped, query_left, query_right, train_left, train_right):
    rank_width = query_right.shape[1]
    basis_rows = basis_out
    rot_left = dot_first(
        basis_rows, lax.all_gather(query_left, "col", axis=0, tiled=True).astype(jnp.float32)
    )
    rot_left = lax.psum(rot_left, "row")
    joined = jnp.concatenate([query_right, train_right], axis=1).astype(jnp.float32)
    share = lax.psum_scatter(dot_first(basis_in, joined), "col", scatter_dimension=0, tiled=True)
    piece = lax.all_gather(share, "col", axis=0, tiled=True)
    precond = dot_last(rot_left, piece[:, :rank_width]) / eig_damped
    contrib = dot_plain(precond, piece[:, rank_width:])
    applied = lax.psum(contrib, "row")
    basis_rows = basis_out
    response = lax.psum_scatter(
        dot_plain(basis_rows, applied), "col", scatter_dimension=0, tiled=True
    )
    partial_scores = jnp.sum(train_left.astype(jnp.float32) * response, axis=0)
    scores = lax.psum(partial_scores, ("row", "col"))
    return (response, scores)


def solution(mesh):
    return jax.shard_map(
        body,
        mesh=mesh,
        in_specs=(
            P("row", "col"),
            P("col", "row"),
            P("col", "row"),
            P(("row", "col"), None),
            P("col", None),
            P(("row", "col"), None),
            P("col", None),
        ),
        out_specs=(P(("row", "col"), None), P()),
        check_vma=False,
    )
```

profile of v0, /device:TPU:6, one launch (start us, length us, event | category | flops | bytes accessed | tf_op | source)
XLA Modules:
  0.0 1388.7 jit_solution(18295817856563887939)
XLA Ops:
  7.2 0.0 all-gather.3.cloned.1.call-start
  7.2 0.7 all-gather.3.cloned.1.call-update
  7.9 0.0 reduce-scatter.3.cloned.1.call-start
  7.9 47.3 %convolution_bitcast_fusion = f32[8192,768]{0,1:T(8,128)} fusion(f32[1024,8192]{1,0:T(8,128)} %param.8, bf16[1024,512]{1,0:T(8,128)(2,1)} %param.13, bf16[1024,256]{1,0:T(8,128)(2,1)} %param.11), kind=kOutput, calls=%fused_computation.3 | convolution fusion | flops 77312557056 | bytes 60293120 | tf_op jit(solution)/shard_map/dot_general | solution.py:8
  55.3 0.0 reduce-scatter.3.cloned.1.call-update
  55.3 0.0 all-reduce.3.cloned.1.call-start
  55.4 31.8 %all-gather.3.cloned.1.call-done = bf16[8192,256]{1,0:T(8,128)(2,1)} async-done(((bf16[512,256]{1,0:T(8,128)(2,1)}), bf16[8192,256]{1,0:T(8,128)(2,1)}) %all-gather.3.cloned.1.call-update) | async-done | bytes 4194320 | tf_op jit(solution)/shard_map/all_gather | solution.py:35
  87.2 43.6 %fusion.9 = f32[1024,256]{1,0:T(8,128)} fusion(f32[8192,1024]{1,0:T(8,128)} %param.7, bf16[8192,256]{1,0:T(8,128)(2,1)} %all-gather.3.cloned.1.call-done), kind=kOutput, calls=%fused_computation.12 | convolution fusion | flops 25769803776 | bytes 38797312 | tf_op jit(solution)/shard_map/dot_general | solution.py:8
  130.8 0.0 all-reduce.3.cloned.1.call-update
  130.8 0.0 all-gather.5.cloned.1.call-start
  130.9 323.6 %reduce-scatter.3.cloned.1.call-done = f32[512,768]{0,1:T(8,128)} async-done(((f32[8192,768]{0,1:T(8,128)}), f32[512,768]{0,1:T(8,128)}) %reduce-scatter.3.cloned.1.call-update) | async-done | bytes 1572880 | tf_op jit(solution)/shard_map/reduce_scatter | solution.py:39
  454.4 0.0 all-reduce.5.cloned.1.call-start
  454.5 21.7 %all-reduce.3.cloned.1.call-done = f32[1024,256]{1,0:T(8,128)} async-done(((f32[1024,256]{1,0:T(8,128)}), f32[1024,256]{1,0:T(8,128)}) %all-reduce.3.cloned.1.call-update) | async-done | bytes 1048592 | tf_op jit(solution)/shard_map/psum | solution.py:37
  476.2 283.2 %all-gather.5.cloned.1.call-done = f32[8192,768]{0,1:T(8,128)} async-done(((f32[512,768]{0,1:T(8,128)}), f32[8192,768]{0,1:T(8,128)}) %all-gather.5.cloned.1.call-update) | async-done | bytes 25165840 | tf_op jit(solution)/shard_map/all_gather | solution.py:40
  759.4 32.3 %fusion.3 = f32[1024,8192]{1,0:T(8,128)} fusion(f32[1024,256]{1,0:T(8,128)} %all-reduce.3.cloned.1.call-done, f32[8192,768]{0,1:T(8,128)} %all-gather.5.cloned.1.call-done), kind=kOutput, calls=%fused_computation.5 | convolution fusion | flops 25769803776 | bytes 42991616 | tf_op jit(solution)/shard_map/dot_general | solution.py:18
  791.7 60.3 %fusion = f32[1024,512]{1,0:T(8,128)} fusion(f32[1024,8192]{1,0:T(8,128)} %fusion.3, f32[1024,8192]{1,0:T(8,128)} %param.9, f32[8192,768]{0,1:T(8,128)S(1)} %copy-done), kind=kOutput, calls=%fused_computation | convolution fusion | flops 51547996160 | bytes 85983232 | tf_op jit(solution)/shard_map/dot_general | solution.py:28
  852.0 0.0 reduce-scatter.5.cloned.1.call-start
  852.1 20.7 %all-reduce.5.cloned.1.call-done = f32[1024,512]{1,0:T(8,128)} async-done(((f32[1024,512]{1,0:T(8,128)}), f32[1024,512]{1,0:T(8,128)}) %all-reduce.5.cloned.1.call-update) | async-done | bytes 2097168 | tf_op jit(solution)/shard_map/psum | solution.py:43
  872.8 111.3 %convolution_bitcast_fusion.1 = f32[8192,512]{0,1:T(8,128)} fusion(f32[1024,512]{1,0:T(8,128)} %all-reduce.5.cloned.1.call-done, f32[8192,1024]{1,0:T(8,128)} %param.7), kind=kOutput, calls=%fused_computation.4 | convolution fusion | flops 51539607552 | bytes 52428800 | tf_op jit(solution)/shard_map/dot_general | solution.py:28
  984.1 0.2 copy.9
  984.3 347.2 %reduce-scatter.5.cloned.1.call-done = f32[512,512]{0,1:T(8,128)} async-done(((f32[8192,512]{0,1:T(8,128)}), f32[512,512]{0,1:T(8,128)}) %reduce-scatter.5.cloned.1.call-update) | async-done | bytes 1048592 | tf_op jit(solution)/shard_map/reduce_scatter | solution.py:45
  1331.5 1.4 multiply_reduce_fusion
  1332.9 46.1 %psum.23 = f32[512]{0:T(512)} all-reduce(f32[512]{0:T(512)S(1)} %multiply_reduce_fusion), channel_id=1, replica_groups=mesh['row'=2,'col'=16] {'row','col'}, use_global_device_ids=true, to_apply=%region_5.0 | all-reduce | flops 512 | bytes 4096 | tf_op jit(solution)/shard_map/psum | solution.py:49
  1378.9 2.5 copy.10
  (7 shorter events, 0.1 us)
Async XLA Ops:
  7.2 80.0 %all-gather.3.cloned.1.call-start = ((), (), s32[]{:S(2)}) async-start(), calls=%async_computation.2 | async-start | bytes 4456448 | tf_op jit(solution)/shard_map/all_gather | solution.py:35
  7.9 446.5 %reduce-scatter.3.cloned.1.call-start = ((), (), s32[]{:S(2)}) async-start(), calls=%async_computation.4 | async-start | bytes 26738688 | tf_op jit(solution)/shard_map/reduce_scatter | solution.py:39
  55.3 420.9 %all-reduce.3.cloned.1.call-start = ((), (), s32[]{:S(2)}) async-start(), calls=%async_computation.3 | async-start | bytes 2097152 | tf_op jit(solution)/shard_map/psum | solution.py:37
  130.8 628.6 %all-gather.5.cloned.1.call-start = ((), (), s32[]{:S(2)}) async-start(), calls=%async_computation.5 | async-start | bytes 26738688 | tf_op jit(solution)/shard_map/all_gather | solution.py:40
  454.4 418.3 %all-reduce.5.cloned.1.call-start = ((), (), s32[]{:S(2)}) async-start(), calls=%async_computation.6 | async-start | bytes 4194304 | tf_op jit(solution)/shard_map/psum | solution.py:43
  759.4 32.3 %copy-start = (f32[8192,768]{0,1:T(8,128)S(1)}, f32[8192,768]{0,1:T(8,128)}, u32[]{:S(2)}) copy-start(f32[8192,768]{0,1:T(8,128)} %all-gather.5.cloned.1.call-done) | copy-start | bytes 75497472
  852.0 132.0 %copy-start.1 = (bf16[512,512]{1,0:T(8,128)(2,1)S(1)}, bf16[512,512]{1,0:T(8,128)(2,1)}, u32[]{:S(2)}) copy-start(bf16[512,512]{1,0:T(8,128)(2,1)} %param.12) | copy-start | bytes 1572868
  852.0 479.4 %reduce-scatter.5.cloned.1.call-start = ((), (), s32[]{:S(2)}) async-start(), calls=%async_computation.7 | async-start | bytes 17825792 | tf_op jit(solution)/shard_map/reduce_scatter | solution.py:45
Sparse Core Ops, SparseCore 0:
  10.8 76.3 all-gather.2
  92.9 361.4 reduce-scatter.2
  457.3 18.8 all-reduce.2
  479.2 280.1 all-gather.4
  852.1 20.5 all-reduce.4
  984.2 347.2 reduce-scatter.4
where the time goes:
time: 1400 us; the launch traced here: 1390 us
  waiting for transfers between devices  1030 us (74%)
  matrix products  295 us (21%)
  blocking collectives  46.1 us (3%)
  between operations  14.5 us (1%)
    reduce_scatter x1, waiting for transfers between devices, body(): lax.psum_scatter(dot_plain(basis_rows, applied), 'col', scatter_dimension...  347 us
    reduce_scatter x1, waiting for transfers between devices, body(): lax.psum_scatter(dot_first(basis_in, joined), 'col', scatter_dimension=0,...  324 us
    all_gather x1, waiting for transfers between devices, body(): piece = lax.all_gather(share, 'col', axis=0, tiled=True)  283 us
    dot_general x2, matrix products, dot_plain(): jnp.dot(left, right, precision=lax.Precision.HIGHEST, preferred_element_t...  172 us
    dot_general x2, matrix products, dot_first(): lax.dot_general(left, right, (((0,), (0,)), ((), ())), precision=lax.Prec...  91 us
    psum x1, blocking collectives, body(): scores = lax.psum(partial_scores, ('row', 'col'))  46.1 us
    dot_general x1, matrix products, dot_last(): lax.dot_general(left, right, (((1,), (1,)), ((), ())), precision=lax.Prec...  32.3 us
    all_gather x1, waiting for transfers between devices, body(): lax.all_gather(query_left, 'col', axis=0, tiled=True).astype(jnp.float32)  31.8 us
  transfers between devices with their start and end apart: 6, of which 6 were waited for; matrix products, arithmetic and copies ran while one was open for 7% of the time, Pallas kernels for 0%

commit v1 on v0

v1 whole, which is shorter than its diff:
```python
import jax
import jax.numpy as jnp
from jax import lax
from jax.sharding import PartitionSpec as P

SPAN = 240.0


def dot(left, right, contract):
    return lax.dot_general(
        left,
        right,
        (contract, ((), ())),
        precision=lax.Precision.HIGH,
        preferred_element_type=jnp.float32,
    )


def encode(x):
    peak = jnp.maximum(jnp.max(jnp.abs(x), axis=-2, keepdims=True), 1e-30)
    size = jnp.exp2(jnp.abs(x) * (SPAN / peak) - SPAN / 2)
    return jnp.where(x < 0, -size, size).astype(jnp.bfloat16), peak


def decode(code, peak):
    code = code.astype(jnp.float32)
    size = (jnp.log2(jnp.abs(code)) + SPAN / 2) * (peak / SPAN)
    return jnp.where(code < 0, -size, size)


def swap(x, axis, devices, bit):
    pairs = [(i, i ^ (1 << bit)) for i in range(devices)]
    return lax.ppermute(x, axis, pairs)


def halving_sum(x, axis, devices, order):
    bits = devices.bit_length() - 1
    me = lax.axis_index(axis)
    x = x.reshape((2,) * bits + (x.shape[0] // devices, x.shape[1]))
    left = list(range(bits - 1, -1, -1))
    for bit in order:
        place = left.index(bit)
        mine = (me >> bit) & 1
        keep = lax.dynamic_index_in_dim(x, mine, place, keepdims=False)
        send = lax.dynamic_index_in_dim(x, 1 - mine, place, keepdims=False)
        code, peak = encode(send)
        x = keep + decode(swap(code, axis, devices, bit), swap(peak, axis, devices, bit))
        left.remove(bit)
    return x


def gather(x, axis, devices):
    code, peak = encode(x)
    code = lax.all_gather(code, axis, axis=0, tiled=False)
    peak = lax.all_gather(peak, axis, axis=0, tiled=False)
    return decode(code, peak).reshape(devices * x.shape[0], x.shape[1])


def make_body(rows, cols):
    bits = cols.bit_length() - 1
    orders = [list(range(bits)), [b ^ 1 if (b ^ 1) < bits else b for b in range(bits)]]

    def body(basis_out, basis_in, eig_damped, query_left, query_right, train_left, train_right):
        rank = query_right.shape[1]
        joined = jnp.concatenate([query_right, train_right], axis=1).astype(jnp.float32)
        half = joined.shape[1] // 2
        shares = []
        for k in range(2):
            part = dot(basis_in, joined[:, k * half : (k + 1) * half], ((0,), (0,)))
            shares.append(halving_sum(part, "col", cols, orders[k]))
        share = jnp.concatenate(shares, axis=1)
        left_all = lax.all_gather(query_left, "col", axis=0, tiled=True)
        rot_left = lax.psum(dot(basis_out, left_all.astype(jnp.float32), ((0,), (0,))), "row")
        rot_right = gather(share[:, :rank], "col", cols)
        rot_train = gather(share[:, rank:], "col", cols)
        precond = dot(rot_left, rot_right, ((1,), (1,))) / eig_damped
        applied = lax.psum(dot(precond, rot_train, ((1,), (0,))), "row")
        half = applied.shape[1] // 2
        pieces = []
        for k in range(2):
            part = dot(basis_out, applied[:, k * half : (k + 1) * half], ((1,), (0,)))
            pieces.append(halving_sum(part, "col", cols, orders[k]))
        response = jnp.concatenate(pieces, axis=1)
        scores = jnp.sum(train_left.astype(jnp.float32) * response, axis=0)
        for bit in range(bits):
            scores = scores + swap(scores, "col", cols, bit)
        for bit in range(rows.bit_length() - 1):
            scores = scores + swap(scores, "row", rows, bit)
        return response, scores

    return body


def solution(mesh):
    return jax.shard_map(
        make_body(mesh.shape["row"], mesh.shape["col"]),
        mesh=mesh,
        in_specs=(
            P("row", "col"),
            P("col", "row"),
            P("col", "row"),
            P(("row", "col"), None),
            P("col", None),
            P(("row", "col"), None),
            P("col", None),
        ),
        out_specs=(P(("row", "col"), None), P()),
        check_vma=False,
    )
```

time: 1400 us -> 956 us (0.68)
  waiting for transfers between devices: 1030 us -> 350 us
  local copies, waits for them, and re-layouts: 2.75 us -> 167 us
  other arithmetic: 1.4 us -> 102 us
  matrix products: 295 us -> 196 us
  starting transfers between devices: 0.24 us -> 40.4 us
  blocking collectives: 46.1 us -> 72.4 us
    reduce_scatter x2 -> x0, waiting for transfers between devices: 671 us -> none  [the longest x1 347 us: body(): lax.psum_scatter(dot_plain(basis_rows, applied), 'col', scatter_dimension...]
    ppermute x0 -> x37, waiting for transfers between devices: none -> 304 us  [swap(): return lax.ppermute(x, axis, pairs)]
    all_gather x2 -> x3, waiting for transfers between devices: 315 us -> 25.3 us  [the longest x2 25.3 us: gather(): code = lax.all_gather(code, axis, axis=0, tiled=False)]
    dot_general x5 -> x7, matrix products: 295 us -> 196 us  [dot(): lax.dot_general(left, right, (contract, ((), ())), precision=lax.Precisio...]
    dynamic_slice x0 -> x7, local copies, waits for them, and re-layouts: none -> 82.6 us  [halving_sum(): keep = lax.dynamic_index_in_dim(x, mine, place, keepdims=False)]
    all_gather x0 -> x2, blocking collectives: none -> 72.4 us  [gather(): peak = lax.all_gather(peak, axis, axis=0, tiled=False)]
    psum x1 -> x0, blocking collectives: 46.1 us -> none  [body(): scores = lax.psum(partial_scores, ('row', 'col'))]
    add x0 -> x23, other arithmetic: none -> 43.6 us  [the longest x16 28.8 us: halving_sum(): keep + decode(swap(code, axis, devices, bit), swap(peak, axis, devices, b...]
  transfers between devices with their start and end apart: 6 -> 42, of which waited for: 6 -> 25; matrix products, arithmetic and copies ran while one was open for 7% -> 26% of each run, Pallas kernels for 0% -> 0%
where the time goes in v1:
time: 956 us; the launch traced here: 943 us
  waiting for transfers between devices  350 us (37%)
  matrix products  196 us (21%)
  local copies, waits for them, and re-layouts  167 us (17%)
  other arithmetic  102 us (11%)
  blocking collectives  72.4 us (8%)
  starting transfers between devices  40.4 us (4%)
  between operations  14.6 us (2%)
    ppermute x37, waiting for transfers between devices, swap(): return lax.ppermute(x, axis, pairs)  304 us
    dot_general x7, matrix products, dot(): lax.dot_general(left, right, (contract, ((), ())), precision=lax.Precisio...  196 us
    dynamic_slice x7, local copies, waits for them, and re-layouts, halving_sum(): keep = lax.dynamic_index_in_dim(x, mine, place, keepdims=False)  82.6 us
    all_gather x2, blocking collectives, gather(): peak = lax.all_gather(peak, axis, axis=0, tiled=False)  72.4 us
    unnamed x31, local copies, waits for them, and re-layouts  43.6 us
    reshape x3, local copies, waits for them, and re-layouts, halving_sum(): x = x.reshape((2,) * bits + (x.shape[0] // devices, x.shape[1]))  40.5 us
    ppermute x37, starting transfers between devices, swap(): return lax.ppermute(x, axis, pairs)  40 us
    add x16, other arithmetic, halving_sum(): keep + decode(swap(code, axis, devices, bit), swap(peak, axis, devices, b...  28.8 us
  transfers between devices with their start and end apart: 42, of which 25 were waited for; matrix products, arithmetic and copies ran while one was open for 26% of the time, Pallas kernels for 0%

profile of v1, /device:TPU:6, one launch (start us, length us, event | category | flops | bytes accessed | tf_op | source)
XLA Modules:
  0.0 942.9 jit_solution(8708562690692126243)
XLA Ops:
  7.2 22.2 %convolution_bitcast_fusion = f32[8192,384]{0,1:T(8,128)} fusion(f32[1024,8192]{1,0:T(8,128)} %param.8, bf16[1024,512]{1,0:T(8,128)(2,1)} %param.13, bf16[1024,256]{1,0:T(8,128)(2,1)} %param.11), kind=kOutput, calls=%fused_computation.9 | convolution fusion | flops 19328925696 | bytes 47710208 | tf_op jit(solution)/shard_map/dot_general | solution.py:10
  29.4 16.9 %reshape.326 = f32[2,2,2,2,512,384]{4,3,2,1,0,5:T(2,128)} reshape(f32[8192,384]{0,1:T(8,128)} %convolution_bitcast_fusion) | data formatting | bytes 25165824 | tf_op jit(solution)/shard_map/reshape | solution.py:39
  46.3 17.1 %constant_dynamic-slice_fusion.7 = (f32[2,2,2,1,512,384]{4,3,2,1,0,5:T(1,128)}, f32[2,2,2,1,512,384]{4,3,2,1,0,5:T(1,128)}) fusion(f32[2,2,2,2,512,384]{4,3,2,1,0,5:T(2,128)} %reshape.326, s32[]{:T(128)S(6)} %select_n.179, s32[]{:T(128)S(6)} %select_n.180), kind=kLoop, calls=%fused_computation.299 | loop fusion | bytes 25165832 | tf_op jit(solution)/shard_map/jit(dynamic_index_in_dim)/dynamic_slice | solution.py:44
  63.4 15.9 %copy.31 = f32[2,2,2,1,512,384]{5,4,0,1,2,3:T(8,128)} copy(f32[2,2,2,1,512,384]{4,3,2,1,0,5:T(1,128)} %get-tuple-element.5) | data formatting | bytes 12582912
  88.3 16.0 %copy.19 = f32[2,2,2,1,512,384]{5,4,0,1,2,3:T(8,128)} copy(f32[2,2,2,1,512,384]{4,3,2,1,0,5:T(1,128)} %get-tuple-element.4) | data formatting | bytes 12582912 | tf_op jit(solution)/shard_map/jit(dynamic_index_in_dim)/dynamic_slice | solution.py:44
  104.3 76.1 %collective-permute-done.1 = f32[2,2,2,1,384]{4,0,1,2,3:T(2,128)S(1)} collective-permute-done((f32[2,2,2,1,384]{4,0,1,2,3:T(2,128)S(1)}, f32[2,2,2,1,384]{4,0,1,2,3:T(2,128)S(1)}, u32[]{:S(2)}, u32[]{:S(2)}) %collective-permute-start.1) | collective-permute-done | bytes 12320 | tf_op jit(solution)/shard_map/ppermute | solution.py:33
  190.6 25.1 %fusion.143 = f32[8192,384]{1,0:T(8,128)} fusion(f32[1024,8192]{1,0:T(8,128)} %param.8, bf16[1024,512]{1,0:T(8,128)(2,1)S(1)} %copy-done.8), kind=kOutput, calls=%fused_computation.246 | convolution fusion | flops 19327352832 | bytes 46923776 | tf_op jit(solution)/shard_map/dot_general | solution.py:10
  259.3 14.3 %collective-permute-done.7 = f32[1,384]{1,0:T(1,128)S(1)} collective-permute-done((f32[1,384]{1,0:T(1,128)S(1)}, f32[1,384]{1,0:T(1,128)S(1)}, u32[]{:S(2)}, u32[]{:S(2)}) %collective-permute-start.7) | collective-permute-done | bytes 1568 | tf_op jit(solution)/shard_map/ppermute | solution.py:33
  277.6 36.9 %collective-permute-done.9 = f32[2,2,2,1,384]{4,0,1,2,3:T(2,128)S(1)} collective-permute-done((f32[2,2,2,1,384]{4,0,1,2,3:T(2,128)S(1)}, f32[2,2,2,1,384]{4,0,1,2,3:T(2,128)S(1)}, u32[]{:S(2)}, u32[]{:S(2)}) %collective-permute-start.9) | collective-permute-done | bytes 12320 | tf_op jit(solution)/shard_map/ppermute | solution.py:33
  322.8 42.7 %collective-permute-done.11 = f32[2,2,1,384]{3,0,1,2:T(2,128)S(1)} collective-permute-done((f32[2,2,1,384]{3,0,1,2:T(2,128)S(1)}, f32[2,2,1,384]{3,0,1,2:T(2,128)S(1)}, u32[]{:S(2)}, u32[]{:S(2)}) %collective-permute-start.11) | collective-permute-done | bytes 6176 | tf_op jit(solution)/shard_map/ppermute | solution.py:33
  370.2 31.3 %collective-permute-done.13 = f32[2,1,384]{2,0,1:T(2,128)S(1)} collective-permute-done((f32[2,1,384]{2,0,1:T(2,128)S(1)}, f32[2,1,384]{2,0,1:T(2,128)S(1)}, u32[]{:S(2)}, u32[]{:S(2)}) %collective-permute-start.13) | collective-permute-done | bytes 3104 | tf_op jit(solution)/shard_map/ppermute | solution.py:33
  402.6 25.8 %fusion.166 = f32[1024,256]{1,0:T(8,128)} fusion(f32[8192,1024]{1,0:T(8,128)} %param.7, bf16[8192,256]{1,0:T(8,128)(2,1)} %all-gather.10.cloned.1.call-done), kind=kOutput, calls=%fused_computation.345 | convolution fusion | flops 12884901888 | bytes 38797312 | tf_op jit(solution)/shard_map/dot_general | solution.py:10
  433.7 33.4 %all-gather.4 = f32[16,1,256]{2,1,0:T(1,128)S(1)} all-gather(f32[1,1,256]{2,1,0:T(1,128)S(1)} %bitcast.350), channel_id=3, replica_groups=mesh['row'=2,'col'=16] {'col'}, dimensions={0}, use_global_device_ids=true | all-gather | bytes 17408 | tf_op jit(solution)/shard_map/all_gather | solution.py:55
  467.2 39.0 %all-gather.5 = f32[16,1,512]{2,1,0:T(1,128)S(1)} all-gather(f32[1,1,512]{2,1,0:T(1,128)S(1)} %bitcast.349), channel_id=5, replica_groups=mesh['row'=2,'col'=16] {'col'}, dimensions={0}, use_global_device_ids=true | all-gather | bytes 34816 | tf_op jit(solution)/shard_map/all_gather | solution.py:55
  517.0 22.1 %fusion.167 = f32[1024,8192]{1,0:T(8,128)} fusion(f32[1024,256]{1,0:T(8,128)} %all-reduce.3.cloned.1.call-done, f32[8192,256]{1,0:T(8,128)} %bitcast.343), kind=kOutput, calls=%fused_computation.346 | convolution fusion | flops 12884901888 | bytes 42991616 | tf_op jit(solution)/shard_map/dot_general | solution.py:10
  539.1 25.3 %all-gather.14.cloned.1.call-done = bf16[8192,512]{1,0:T(8,128)(2,1)} async-done(((bf16[512,512]{1,0:T(8,128)(2,1)}), bf16[8192,512]{1,0:T(8,128)(2,1)}) %all-gather.14.cloned.1.call-update) | async-done | bytes 8388624 | tf_op jit(solution)/shard_map/all_gather | solution.py:54
  570.5 12.5 %fusion.4 = f32[8192,512]{1,0:T(8,128)} fusion(bf16[8192,512]{1,0:T(8,128)(2,1)} %all-gather.14.cloned.1.call-done), kind=kLoop, calls=%fused_computation.7 | loop fusion | flops 16777216 | bytes 25165824 | tf_op jit(solution)/shard_map/add | solution.py:27
  595.3 35.5 %fusion = f32[1024,512]{1,0:T(8,128)} fusion(f32[8192,512]{1,0:T(8,128)} %bitcast.344, f32[1024,8192]{1,0:T(8,128)} %fusion.167, f32[1024,8192]{1,0:T(8,128)} %param.9), kind=kOutput, calls=%fused_computation | convolution fusion | flops 25778192384 | bytes 85983232 | tf_op jit(solution)/shard_map/dot_general | solution.py:10
  630.8 20.7 %all-reduce.5.cloned.1.call-done = f32[1024,512]{1,0:T(8,128)} async-done(((f32[1024,512]{1,0:T(8,128)}), f32[1024,512]{1,0:T(8,128)}) %all-reduce.5.cloned.1.call-update) | async-done | bytes 2097168 | tf_op jit(solution)/shard_map/psum | solution.py:77
  651.5 32.0 %convolution_bitcast_fusion.1 = f32[8192,256]{0,1:T(8,128)} fusion(f32[8192,1024]{1,0:T(8,128)} %param.7, f32[1024,512]{1,0:T(8,128)} %all-reduce.5.cloned.1.call-done), kind=kOutput, calls=%fused_computation.10 | convolution fusion | flops 12884901888 | bytes 42991616 | tf_op jit(solution)/shard_map/dot_general | solution.py:10
  720.5 33.6 %convolution_bitcast_fusion.2 = f32[8192,256]{0,1:T(8,128)} fusion(f32[8192,1024]{1,0:T(8,128)} %param.7, f32[1024,512]{1,0:T(8,128)S(1)} %copy-done.9), kind=kOutput, calls=%fused_computation.11 | convolution fusion | flops 12884901888 | bytes 42991616 | tf_op jit(solution)/shard_map/dot_general | solution.py:10
  765.9 12.4 %constant_dynamic-slice_fusion.3 = (f32[2,2,2,1,512,256]{4,3,2,1,0,5:T(1,128)}, f32[2,2,2,1,512,256]{4,3,2,1,0,5:T(1,128)}) fusion(f32[2,2,2,2,512,256]{4,3,2,1,0,5:T(2,128)} %reshape.330, s32[]{:T(128)S(6)} %select_n.179, s32[]{:T(128)S(6)} %select_n.180), kind=kLoop, calls=%fused_computation.295 | loop fusion | bytes 16777224 | tf_op jit(solution)/shard_map/jit(dynamic_index_in_dim)/dynamic_slice | solution.py:44
  815.9 26.1 %collective-permute-done.17 = f32[2,2,2,1,256]{4,0,1,2,3:T(2,128)S(1)} collective-permute-done((f32[2,2,2,1,256]{4,0,1,2,3:T(2,128)S(1)}, f32[2,2,2,1,256]{4,0,1,2,3:T(2,128)S(1)}, u32[]{:S(2)}, u32[]{:S(2)}) %collective-permute-start.17) | collective-permute-done | bytes 8224 | tf_op jit(solution)/shard_map/ppermute | solution.py:33
  856.3 15.3 %collective-permute-done.26 = bf16[2,2,512,256]{3,2,0,1:T(8,128)(2,1)S(1)} collective-permute-done((bf16[2,2,512,256]{3,2,0,1:T(8,128)(2,1)S(1)}, bf16[2,2,512,256]{3,2,0,1:T(8,128)(2,1)S(1)}, u32[]{:S(2)}, u32[]{:S(2)}) %collective-permute-start.26) | collective-permute-done | bytes 1048608 | tf_op jit(solution)/shard_map/ppermute | solution.py:33
  (218 shorter events, 280.1 us)
Async XLA Ops:
  7.2 395.4 %all-gather.10.cloned.1.call-start = ((), (), s32[]{:S(2)}) async-start(), calls=%async_computation | async-start | bytes 4456448 | tf_op jit(solution)/shard_map/all_gather | solution.py:72
  85.9 94.5 %collective-permute-start = (bf16[2,2,2,512,384]{4,3,0,1,2:T(8,128)(2,1)S(1)}, bf16[2,2,2,512,384]{4,3,0,1,2:T(8,128)(2,1)}, u32[]{:S(2)}, u32[]{:S(2)}) collective-permute-start(bf16[2,2,2,512,384]{4,3,0,1,2:T(8,128)(2,1)S(1)} %fusion.16), channel_id=1, source_target_pairs={{0,1},{1,0},{2,3},{3,2},{4,5},{5,4},{6,7},{7,6},{8,9},{9,8},{10,11... | collective-permute-start | bytes 9437192 | tf_op jit(solution)/shard_map/ppermute | solution.py:33
  86.5 93.8 %collective-permute-start.1 = (f32[2,2,2,1,384]{4,0,1,2,3:T(2,128)S(1)}, f32[2,2,2,1,384]{4,0,1,2,3:T(2,128)S(1)}, u32[]{:S(2)}, u32[]{:S(2)}) collective-permute-start(f32[2,2,2,1,384]{4,0,1,2,3:T(2,128)S(1)} %get-tuple-element.12), channel_id=1, source_target_pairs={{0,1},{1,0},{2,3},{3,2},{4,5},{5,4},{6,7},{7,6},{8,9},{9,8},{10,11... | collective-permute-start | bytes 36872 | tf_op jit(solution)/shard_map/ppermute | solution.py:33
  88.1 418.2 %all-gather.12.cloned.1.call-start = ((), (), s32[]{:S(2)}) async-start(), calls=%async_computation.3 | async-start | bytes 4456448 | tf_op jit(solution)/shard_map/all_gather | solution.py:54
  190.1 40.4 %collective-permute-start.2 = (bf16[2,2,512,384]{3,2,0,1:T(8,128)(2,1)}, bf16[2,2,512,384]{3,2,0,1:T(8,128)(2,1)}, u32[]{:S(2)}, u32[]{:S(2)}) collective-permute-start(bf16[2,2,512,384]{3,2,0,1:T(8,128)(2,1)} %fusion.53), channel_id=1, source_target_pairs={{0,2},{1,3},{2,0},{3,1},{4,6},{5,7},{6,4},{7,5},{8,10},{9,11},{10,... | collective-permute-start | bytes 4718600 | tf_op jit(solution)/shard_map/ppermute | solution.py:33
  235.7 17.4 %collective-permute-start.4 = (bf16[2,512,384]{2,1,0:T(8,128)(2,1)}, bf16[2,512,384]{2,1,0:T(8,128)(2,1)}, u32[]{:S(2)}, u32[]{:S(2)}) collective-permute-start(bf16[2,512,384]{2,1,0:T(8,128)(2,1)} %fusion.89), channel_id=1, source_target_pairs={{0,4},{1,5},{2,6},{3,7},{4,0},{5,1},{6,2},{7,3},{8,12},{9,13},{10,... | collective-permute-start | bytes 2359304 | tf_op jit(solution)/shard_map/ppermute | solution.py:33
  241.0 73.5 %collective-permute-start.8 = (bf16[2,2,2,512,384]{4,3,0,1,2:T(8,128)(2,1)}, bf16[2,2,2,512,384]{4,3,0,1,2:T(8,128)(2,1)}, u32[]{:S(2)}, u32[]{:S(2)}) collective-permute-start(bf16[2,2,2,512,384]{4,3,0,1,2:T(8,128)(2,1)} %fusion.18), channel_id=1, source_target_pairs={{0,2},{1,3},{2,0},{3,1},{4,6},{5,7},{6,4},{7,5},{8,10},{9,11},{10,... | collective-permute-start | bytes 9437192 | tf_op jit(solution)/shard_map/ppermute | solution.py:33
  276.0 241.1 %all-reduce.3.cloned.1.call-start = ((), (), s32[]{:S(2)}) async-start(), calls=%async_computation.1 | async-start | bytes 2097152 | tf_op jit(solution)/shard_map/psum | solution.py:73
  276.0 38.5 %collective-permute-start.9 = (f32[2,2,2,1,384]{4,0,1,2,3:T(2,128)S(1)}, f32[2,2,2,1,384]{4,0,1,2,3:T(2,128)S(1)}, u32[]{:S(2)}, u32[]{:S(2)}) collective-permute-start(f32[2,2,2,1,384]{4,0,1,2,3:T(2,128)S(1)} %get-tuple-element.14), channel_id=1, source_target_pairs={{0,2},{1,3},{2,0},{3,1},{4,6},{5,7},{6,4},{7,5},{8,10},{9,11},{10,... | collective-permute-start | bytes 36872 | tf_op jit(solution)/shard_map/ppermute | solution.py:33
  320.7 44.8 %collective-permute-start.10 = (bf16[2,2,512,384]{3,2,0,1:T(8,128)(2,1)S(1)}, bf16[2,2,512,384]{3,2,0,1:T(8,128)(2,1)S(1)}, u32[]{:S(2)}, u32[]{:S(2)}) collective-permute-start(bf16[2,2,512,384]{3,2,0,1:T(8,128)(2,1)S(1)} %fusion.55), channel_id=1, source_target_pairs={{0,1},{1,0},{2,3},{3,2},{4,5},{5,4},{6,7},{7,6},{8,9},{9,8},{10,11... | collective-permute-start | bytes 4718600 | tf_op jit(solution)/shard_map/ppermute | solution.py:33
  321.3 44.1 %collective-permute-start.11 = (f32[2,2,1,384]{3,0,1,2:T(2,128)S(1)}, f32[2,2,1,384]{3,0,1,2:T(2,128)S(1)}, u32[]{:S(2)}, u32[]{:S(2)}) collective-permute-start(f32[2,2,1,384]{3,0,1,2:T(2,128)S(1)} %get-tuple-element.22), channel_id=1, source_target_pairs={{0,1},{1,0},{2,3},{3,2},{4,5},{5,4},{6,7},{7,6},{8,9},{9,8},{10,11... | collective-permute-start | bytes 18440 | tf_op jit(solution)/shard_map/ppermute | solution.py:33
  367.2 34.3 %collective-permute-start.12 = (bf16[2,512,384]{2,1,0:T(8,128)(2,1)S(1)}, bf16[2,512,384]{2,1,0:T(8,128)(2,1)S(1)}, u32[]{:S(2)}, u32[]{:S(2)}) collective-permute-start(bf16[2,512,384]{2,1,0:T(8,128)(2,1)S(1)} %fusion.91), channel_id=1, source_target_pairs={{0,8},{1,9},{2,10},{3,11},{4,12},{5,13},{6,14},{7,15},{8,0},{9,1},... | collective-permute-start | bytes 2359304 | tf_op jit(solution)/shard_map/ppermute | solution.py:33
  370.1 31.5 %collective-permute-start.13 = (f32[2,1,384]{2,0,1:T(2,128)S(1)}, f32[2,1,384]{2,0,1:T(2,128)S(1)}, u32[]{:S(2)}, u32[]{:S(2)}) collective-permute-start(f32[2,1,384]{2,0,1:T(2,128)S(1)} %get-tuple-element.30), channel_id=1, source_target_pairs={{0,8},{1,9},{2,10},{3,11},{4,12},{5,13},{6,14},{7,15},{8,0},{9,1},... | collective-permute-start | bytes 9224 | tf_op jit(solution)/shard_map/ppermute | solution.py:33
  402.5 29.7 %collective-permute-start.14 = (bf16[512,384]{1,0:T(8,128)(2,1)S(1)}, bf16[512,384]{1,0:T(8,128)(2,1)S(1)}, u32[]{:S(2)}, u32[]{:S(2)}) collective-permute-start(bf16[512,384]{1,0:T(8,128)(2,1)S(1)} %fusion.134), channel_id=1, source_target_pairs={{0,4},{1,5},{2,6},{3,7},{4,0},{5,1},{6,2},{7,3},{8,12},{9,13},{10,... | collective-permute-start | bytes 1179656 | tf_op jit(solution)/shard_map/ppermute | solution.py:33
  428.4 135.9 %all-gather.14.cloned.1.call-start = ((), (), s32[]{:S(2)}) async-start(), calls=%async_computation.4 | async-start | bytes 8912896 | tf_op jit(solution)/shard_map/all_gather | solution.py:54
  433.7 217.8 %all-reduce.5.cloned.1.call-start = ((), (), s32[]{:S(2)}) async-start(), calls=%async_computation.2 | async-start | bytes 4194304 | tf_op jit(solution)/shard_map/psum | solution.py:77
  719.9 122.0 %collective-permute-start.24 = (bf16[2,2,2,512,256]{4,3,0,1,2:T(8,128)(2,1)}, bf16[2,2,2,512,256]{4,3,0,1,2:T(8,128)(2,1)}, u32[]{:S(2)}, u32[]{:S(2)}) collective-permute-start(bf16[2,2,2,512,256]{4,3,0,1,2:T(8,128)(2,1)} %fusion.37), channel_id=1, source_target_pairs={{0,2},{1,3},{2,0},{3,1},{4,6},{5,7},{6,4},{7,5},{8,10},{9,11},{10,... | collective-permute-start | bytes 6291464 | tf_op jit(solution)/shard_map/ppermute | solution.py:33
  794.1 55.2 %collective-permute-start.16 = (bf16[2,2,2,512,256]{4,3,0,1,2:T(8,128)(2,1)S(1)}, bf16[2,2,2,512,256]{4,3,0,1,2:T(8,128)(2,1)}, u32[]{:S(2)}, u32[]{:S(2)}) collective-permute-start(bf16[2,2,2,512,256]{4,3,0,1,2:T(8,128)(2,1)S(1)} %fusion.35), channel_id=1, source_target_pairs={{0,1},{1,0},{2,3},{3,2},{4,5},{5,4},{6,7},{7,6},{8,9},{9,8},{10,11... | collective-permute-start | bytes 6291464 | tf_op jit(solution)/shard_map/ppermute | solution.py:33
  794.5 21.4 %collective-permute-start.25 = (f32[2,2,2,1,256]{4,0,1,2,3:T(2,128)S(1)}, f32[2,2,2,1,256]{4,0,1,2,3:T(2,128)S(1)}, u32[]{:S(2)}, u32[]{:S(2)}) collective-permute-start(f32[2,2,2,1,256]{4,0,1,2,3:T(2,128)S(1)} %get-tuple-element.18), channel_id=1, source_target_pairs={{0,2},{1,3},{2,0},{3,1},{4,6},{5,7},{6,4},{7,5},{8,10},{9,11},{10,... | collective-permute-start | bytes 24584 | tf_op jit(solution)/shard_map/ppermute | solution.py:33
  814.4 27.5 %collective-permute-start.17 = (f32[2,2,2,1,256]{4,0,1,2,3:T(2,128)S(1)}, f32[2,2,2,1,256]{4,0,1,2,3:T(2,128)S(1)}, u32[]{:S(2)}, u32[]{:S(2)}) collective-permute-start(f32[2,2,2,1,256]{4,0,1,2,3:T(2,128)S(1)} %get-tuple-element.16), channel_id=1, source_target_pairs={{0,1},{1,0},{2,3},{3,2},{4,5},{5,4},{6,7},{7,6},{8,9},{9,8},{10,11... | collective-permute-start | bytes 24584 | tf_op jit(solution)/shard_map/ppermute | solution.py:33
  847.5 24.2 %collective-permute-start.26 = (bf16[2,2,512,256]{3,2,0,1:T(8,128)(2,1)S(1)}, bf16[2,2,512,256]{3,2,0,1:T(8,128)(2,1)S(1)}, u32[]{:S(2)}, u32[]{:S(2)}) collective-permute-start(bf16[2,2,512,256]{3,2,0,1:T(8,128)(2,1)S(1)} %fusion.73), channel_id=1, source_target_pairs={{0,1},{1,0},{2,3},{3,2},{4,5},{5,4},{6,7},{7,6},{8,9},{9,8},{10,11... | collective-permute-start | bytes 3145736 | tf_op jit(solution)/shard_map/ppermute | solution.py:33
  854.8 23.6 %collective-permute-start.18 = (bf16[2,2,512,256]{3,2,0,1:T(8,128)(2,1)S(1)}, bf16[2,2,512,256]{3,2,0,1:T(8,128)(2,1)S(1)}, u32[]{:S(2)}, u32[]{:S(2)}) collective-permute-start(bf16[2,2,512,256]{3,2,0,1:T(8,128)(2,1)S(1)} %fusion.71), channel_id=1, source_target_pairs={{0,2},{1,3},{2,0},{3,1},{4,6},{5,7},{6,4},{7,5},{8,10},{9,11},{10,... | collective-permute-start | bytes 3145736 | tf_op jit(solution)/shard_map/ppermute | solution.py:33
  875.5 24.0 %collective-permute-start.28 = (bf16[2,512,256]{2,1,0:T(8,128)(2,1)S(1)}, bf16[2,512,256]{2,1,0:T(8,128)(2,1)S(1)}, u32[]{:S(2)}, u32[]{:S(2)}) collective-permute-start(bf16[2,512,256]{2,1,0:T(8,128)(2,1)S(1)} %fusion.112), channel_id=1, source_target_pairs={{0,8},{1,9},{2,10},{3,11},{4,12},{5,13},{6,14},{7,15},{8,0},{9,1},... | collective-permute-start | bytes 1572872 | tf_op jit(solution)/shard_map/ppermute | solution.py:33
  881.1 22.0 %collective-permute-start.20 = (bf16[2,512,256]{2,1,0:T(8,128)(2,1)S(1)}, bf16[2,512,256]{2,1,0:T(8,128)(2,1)S(1)}, u32[]{:S(2)}, u32[]{:S(2)}) collective-permute-start(bf16[2,512,256]{2,1,0:T(8,128)(2,1)S(1)} %fusion.110), channel_id=1, source_target_pairs={{0,4},{1,5},{2,6},{3,7},{4,0},{5,1},{6,2},{7,3},{8,12},{9,13},{10,... | collective-permute-start | bytes 1572872 | tf_op jit(solution)/shard_map/ppermute | solution.py:33
  (31 other events, 197.6 us)
Sparse Core Ops, SparseCore 0:
  88.2 100.7 all-gather.9
  276.1 111.7 all-gather.11
  428.6 19.5 all-reduce.2
  451.2 113.1 all-gather.13
  630.9 20.5 all-reduce.4
